TPU v7x, 256 devices: a whole 4x4x8 slice. The times are simulated.
256 devices in a mesh: grid: 64 (over z, y, core), chan: 4 (over x).
Axes of the slice: x: 4, y: 4, z: 8, core: 2. Of those that a mesh axis runs over, the one named last changes fastest.
Arguments:
- profiles: bfloat16 [65536, 274], P('grid'), may hold values from -6 to 6
- owner_block: int32 [262144, 1], P(('grid', 'chan')), may hold values from 0 to 63; in each aligned block of 1024 rows (0 to 1023, 1024 to 2047, ...) at most 32 rows name the same one
- column_offset: int32 [262144], P(('grid', 'chan')), may hold values from 0 to 1023
- observed: float32 [262144, 384], P(('grid', 'chan')), may hold values from -8 to 8
- sigma: float32 [384], replicated, may hold values from 0.5 to 2
- qc_flags: int32 [262144, 384], P(('grid', 'chan')), may hold values 0 or 1
- w_first: bfloat16 [274, 512], replicated, may hold values from -0.375 to 0.375
- w_second: bfloat16 [512, 512], replicated, may hold values from -0.25 to 0.25
- w_third: bfloat16 [512, 384], replicated, may hold values from -0.25 to 0.25
Outputs:
- grad_profiles: float32 [65536, 274], P(('grid', 'chan'))
Inputs may be any that keep to these rules, and one draw needn't show every extreme that they name: `owner_block`: in the rows of one device (aligned blocks of 1024 rows) no value appears more than 32 times, and some value appears exactly 32 times.
All inputs are finite; a program needn't handle non-finite values. No bound on the sum of `qc_flags` on one device may be relied on, other than what follows from the above.
Results may differ from a plain program's by a relative error of at most 0.0063.
Values may be sent and summed in bfloat16 or wider, within the bound.
No kernel may reach another device: no remote copies, remote signals or barrier semaphores. Data moves between devices by JAX's collectives and lax.ppermute only.
A program may use at most 128 MiB of HBM per device.

v0:
```python
import functools
import itertools
import math

import jax
import jax.numpy as jnp
from jax import lax
from jax.experimental import pallas as pl
from jax.experimental.pallas import tpu as pltpu
from jax.sharding import PartitionSpec as P

LANES = 128
BASE = 32
AXES = ("zhi", "zlo", "y", "core", "chan")
GROUP = AXES[1:]
GRID = AXES[:-1]


def home(place, places):
    zhi, zlo, y, core, chan = place
    shift = (chan + 2 * core) % places
    return (zhi + shift) % places, zlo ^ int(shift == places // 2), y, core


def devices(sizes):
    return list(itertools.product(*(range(n) for n in sizes)))
F32 = jnp.float32
BF16 = jnp.bfloat16
NT = (((1,), (1,)), ((), ()))


def iota(shape, axis):
    return lax.broadcasted_iota(jnp.int32, shape, axis)


def nn(a, b):
    return jnp.dot(a, b, preferred_element_type=F32)


def nt(a, b):
    return lax.dot_general(a, b, NT, preferred_element_type=F32)


def call(kernel, out, args, vmem=48, **kw):
    return pl.pallas_call(
        kernel,
        out_shape=out,
        compiler_params=pltpu.CompilerParams(vmem_limit_bytes=vmem * 2**20),
        **kw,
    )(*args)


def flat(a):
    return jnp.concatenate([a[r : r + 1, :] for r in range(a.shape[0])], axis=1)


def push_kernel(
    owners,
    cap,
    chunk,
    target_hbm,
    offset_hbm,
    observed_hbm,
    flags_hbm,
    out_hbm,
    target_ref,
    offset_ref,
    observed_ref,
    flags_ref,
    data,
    staged,
    sems,
    out_sems,
):
    pairs = (
        (target_hbm, target_ref),
        (offset_hbm, offset_ref),
        (observed_hbm, observed_ref),
        (flags_hbm, flags_ref),
    )
    gets = [pltpu.make_async_copy(src, dst, sems.at[k]) for k, (src, dst) in enumerate(pairs)]
    for get in gets:
        get.start()
    gets[0].wait()
    gets[1].wait()
    tiles = target_ref.shape[0]
    count = tiles * LANES
    channels = observed_ref.shape[1]
    owner = flat(target_ref[...])
    places = lax.axis_size("zhi")
    near = owners // places
    shift = (owner // near - lax.axis_index("zhi") + places) & (places - 1)
    ring = (shift - 2 * (owner & 1) + places) & (places - 1)
    swap = jnp.where(shift == places // 2, near // 2, 0)
    target = ((owner & (near - 1)) ^ swap) * places + ring
    offset = flat(offset_ref[...])
    hot = jnp.where(iota((owners, count), 0) == target, 1.0, 0.0)
    upper = jnp.where(iota((256, 256), 0) <= iota((256, 256), 1), 1.0, 0.0).astype(BF16)
    carry = jnp.zeros((owners, 1), F32)
    slots = []
    for b in range(count // 256):
        part = hot[:, b * 256 : (b + 1) * 256]
        seen = nn(part.astype(BF16), upper) + carry
        carry = seen[:, 255:256]
        slots.append(jnp.sum(part * (seen - 1.0), axis=0, keepdims=True))
    slot = jnp.concatenate(slots, axis=1)
    place = target * cap + slot.astype(jnp.int32)
    high = offset // BASE
    low = offset - high * BASE
    at_slot = jnp.where((iota((LANES, count), 0) & (cap - 1)).astype(F32) == slot, 1.0, 0.0)
    hot = hot.astype(BF16)
    pair = jnp.concatenate([at_slot * (high + 1).astype(F32), at_slot * low.astype(F32)], axis=0)
    pair = nt(hot, pair.astype(BF16))
    high, low = pair[:, :LANES] - 1.0, pair[:, LANES:]

    gets[2].wait()
    data[:, :channels] = observed_ref[...].astype(BF16)
    gets[3].wait()
    data[:, channels:] = flags_ref[...].astype(F32).astype(BF16)
    parts = 2 * channels // LANES
    puts = []
    for k, s in enumerate(range(0, owners, chunk)):
        put = jnp.where(place - s * cap == iota((chunk * cap, count), 0), 1.0, 0.0).astype(BF16)
        rows = nn(put, data[...]).astype(BF16).reshape(chunk, cap, 2 * channels)
        for j in range(parts):
            staged[s : s + chunk, j * cap : (j + 1) * cap, :] = rows[:, :, j * LANES : (j + 1) * LANES]
        digits = jnp.where(
            iota((chunk, 8, LANES), 1) == 0,
            high[s : s + chunk, :].reshape(chunk, 1, LANES),
            low[s : s + chunk, :].reshape(chunk, 1, LANES),
        )
        staged[s : s + chunk, parts * cap :, :] = digits.astype(BF16)
        puts.append(
            pltpu.make_async_copy(
                staged.at[pl.ds(s, chunk)], out_hbm.at[pl.ds(s, chunk)], out_sems.at[k]
            )
        )
        puts[-1].start()
    for put in puts:
        put.wait()


def forward_kernel(table_ref, w1_ref, w2_ref, w3_ref, evolved_ref, first_ref, second_ref):
    first = jnp.tanh(nn(table_ref[...], w1_ref[...])).astype(BF16)
    second = jnp.tanh(nn(first, w2_ref[...])).astype(BF16)
    first_ref[...] = first
    second_ref[...] = second
    evolved_ref[...] = nn(second, w3_ref[...]).astype(BF16)


def departures_kernel(cap, chunk, arrived_ref, evolved_ref, sigma_ref, out_ref, ids_ref):
    sources = arrived_ref.shape[0]
    cols, channels = evolved_ref.shape
    parts = channels // LANES
    digits = arrived_ref[:, 2 * parts * cap :, :].reshape(sources * 8, LANES)
    row = iota((sources, sources * 8), 1) - 8 * iota((sources, sources * 8), 0)
    high = nn(jnp.where(row == 0, 1.0, 0.0).astype(BF16), digits)
    low = nn(jnp.where(row == 1, 1.0, 0.0).astype(BF16), digits)
    per = LANES // cap
    mine = iota((sources, LANES), 1) // cap == iota((sources, LANES), 0) % per
    gather = jnp.where(
        iota((sources // per, sources), 1) // per == iota((sources // per, sources), 0), 1.0, 0.0
    ).astype(BF16)
    spread = lambda a: nn(gather, jnp.where(mine, a, 0.0).astype(BF16))
    ids_ref[...] = (spread(high) * BASE + spread(low)).astype(jnp.int32)
    column = (high * BASE + low).T
    wide = iota((cap, cols), 1).astype(F32)
    inverse = 1.0 / sigma_ref[...]
    for s in range(0, sources, chunk):
        pick = jnp.concatenate(
            [
                jnp.where(column[:cap, s + j : s + j + 1] == wide, 1.0, 0.0).astype(BF16)
                for j in range(chunk)
            ],
            axis=0,
        )
        evolved = nn(pick, evolved_ref[...])
        for j in range(parts):
            lanes = slice(j * LANES, (j + 1) * LANES)
            take = lambda k: arrived_ref[s : s + chunk, k * cap : (k + 1) * cap, :].reshape(
                chunk * cap, LANES
            ).astype(F32)
            departure = (evolved[:, lanes] - take(j)) * inverse[:, lanes]
            weighted = take(parts + j) * jnp.clip(departure, -1.5, 1.5) * inverse[:, lanes]
            out_ref[s * cap : (s + chunk) * cap, lanes] = weighted.astype(BF16)


def adjoint_kernel(
    shifts, quarter, ids_ref, departures_ref, first_ref, second_ref, w1_ref, w2_ref, w3_ref, *outs
):
    groups = len(shifts)
    each = range(groups)
    which = [lax.rem(lax.axis_index("chan") + k, groups) * quarter for k in shifts]
    rows = [pl.ds(pl.multiple_of(start, quarter), quarter) for start in which]
    ids = flat(ids_ref[...])
    total, grad_second, grad_first = [], [], []
    for k in each:
        put = jnp.where(ids - which[k] == iota((quarter, ids.shape[1]), 0), 1.0, 0.0).astype(BF16)
        total.append(nn(put, departures_ref[...]).astype(BF16))
    for k in each:
        second = second_ref[rows[k], :].astype(F32)
        grad_second.append((nt(total[k], w3_ref[...]) * (1.0 - second * second)).astype(BF16))
    for k in each:
        first = first_ref[rows[k], :].astype(F32)
        grad_first.append((nt(grad_second[k], w2_ref[...]) * (1.0 - first * first)).astype(BF16))
    for k, out_ref in enumerate(outs):
        out_ref[...] = nt(w1_ref[: out_ref.shape[0], :], grad_first[k]).astype(BF16)


def add_kernel(so_far_ref, part_ref, out_ref):
    out_ref[...] = so_far_ref[...].astype(F32) + part_ref[...].astype(F32)


def total_kernel(so_far_ref, part_ref, out_ref):
    total = so_far_ref[...] + part_ref[...].astype(F32)
    out_ref[...] = total[: out_ref.shape[0], :]


def on_device(
    profiles, owner_block, column_offset, observed, sigma, qc_flags, w_first, w_second, w_third
):
    sizes = tuple(lax.axis_size(name) for name in AXES)
    owners = math.prod(sizes[:-1])
    places, groups = sizes[0], sizes[-1]
    everyone = devices(sizes)
    number = {place: i for i, place in enumerate(everyone)}
    rows = owner_block.shape[0]
    cap = 2 * rows // owners
    cols, width = profiles.shape
    hidden, channels = w_third.shape
    quarter = cols // groups
    tiles = rows // LANES
    chunk = 16
    few = 8
    sds = jax.ShapeDtypeStruct
    far = pl.BlockSpec(memory_space=pltpu.HBM)

    def at_home(place, chan):
        return number[(*home(place, places), chan)]

    fetched = lax.ppermute(profiles.T, AXES, [(at_home(p, p[4]), number[p]) for p in everyone])

    bundle = sds((owners, 2 * channels // LANES * cap + 8, LANES), BF16)
    pushed = call(
        functools.partial(push_kernel, owners, cap, few),
        bundle,
        (owner_block.reshape(tiles, LANES), column_offset.reshape(tiles, LANES), observed, qc_flags),
        vmem=62,
        in_specs=[far] * 4,
        out_specs=far,
        scratch_shapes=[
            pltpu.VMEM((tiles, LANES), jnp.int32),
            pltpu.VMEM((tiles, LANES), jnp.int32),
            pltpu.VMEM((rows, channels), F32),
            pltpu.VMEM((rows, channels), jnp.int32),
            pltpu.VMEM((rows, 2 * channels), BF16),
            pltpu.VMEM(bundle.shape, BF16),
            pltpu.SemaphoreType.DMA((4,)),
            pltpu.SemaphoreType.DMA((owners // few,)),
        ],
    )
    arrived = lax.all_to_all(pushed, GROUP, split_axis=0, concat_axis=0, tiled=True)

    padded = -(-width // LANES) * LANES
    wide = lambda a, axis: jnp.pad(a, [(0, padded - width) if k == axis else (0, 0) for k in (0, 1)])
    w1 = wide(w_first, 0)
    evolved, first, second = call(
        forward_kernel,
        (sds((cols, channels), BF16), sds((cols, hidden), BF16), sds((cols, hidden), BF16)),
        (wide(fetched.T, 1), w1, w_second, w_third),
        vmem=24,
        cost_estimate=pl.CostEstimate(flops=10**11, bytes_accessed=4 * 10**6, transcendentals=10**6),
    )

    departures, ids = call(
        functools.partial(departures_kernel, cap, chunk),
        (sds((owners * cap, channels), BF16), sds((owners * cap // LANES, LANES), jnp.int32)),
        (arrived, evolved, sigma.reshape(1, channels)),
        vmem=32,
    )
    order = sorted(range(groups), key=lambda k: -min(k, groups - k))
    gradients = call(
        functools.partial(adjoint_kernel, order, quarter),
        [sds((-(-width // 32) * 32, quarter), BF16)] * groups,
        (ids, departures, first, second, w1, w_second, w_third),
        vmem=32,
        cost_estimate=pl.CostEstimate(flops=8 * 10**9, bytes_accessed=4 * 10**6, transcendentals=0),
    )
    shares = [
        lax.ppermute(part, AXES, [(number[p], at_home(p, (p[4] + k) % groups)) for p in everyone])
        for k, part in zip(order, gradients)
    ]
    total = shares[0]
    for share in shares[1:-1]:
        total = call(
            add_kernel,
            sds(share.shape, F32),
            (total, share),
            vmem=24,
            cost_estimate=pl.CostEstimate(flops=10**10, bytes_accessed=10**6, transcendentals=0),
        )
    return call(total_kernel, sds((width, quarter), F32), (total, shares[-1]), vmem=24).T


def solution(mesh):
    grid, chan = mesh.devices.shape
    places = 4
    near = jax.sharding.Mesh(mesh.devices.reshape(places, 2, grid // (4 * places), 2, chan), AXES)
    whole = P((*GRID, "chan"), None)
    in_specs = (P(GRID, None), whole, P((*GRID, "chan")), whole, P(), whole, P(), P(), P())
    return jax.shard_map(on_device, mesh=near, in_specs=in_specs, out_specs=whole, check_vma=False)
```

profile of v0, /device:TPU:34, one launch (start us, length us, event | category | flops | bytes accessed | tf_op | source)
XLA Modules:
  0.0 93.9 jit_solution(6640865374133393852)
XLA Ops:
  0.0 7.3 %collective-permute-start = (bf16[274,1024]{1,0:T(8,128)(2,1)}, bf16[274,1024]{1,0:T(8,128)(2,1)}, u32[]{:S(2)}, u32[]{:S(2)}) collective-permute-start(bf16[274,1024]{1,0:T(8,128)(2,1)} %bitcast.8), channel_id=1, source_target_pairs={{0,0},{65,1},{162,2},{195,3},{164,4},{197,5},{6,6},{71,7},{8,8},{7... | collective-permute-start | bytes 1683464 | tf_op jit(solution)/shard_map/ppermute | solution.py:241
  7.3 6.2 %shard_map.91 = bf16[64,200,128]{2,1,0:T(8,128)(2,1)} custom-call(s32[8,128]{1,0:T(8,128)} %bitcast.6, s32[8,128]{1,0:T(8,128)} %bitcast.7, f32[1024,384]{1,0:T(8,128)} %observed_hbm.1, s32[1024,384]{1,0:T(8,128)} %flags_hbm.1), custom_call_target="tpu_custom_call" | custom-call | tf_op jit(solution)/shard_map/pallas_call | solution.py:45
  13.5 0.0 copy-start.12
  13.5 9.5 %all-to-all-start = ((bf16[64,200,128]{2,1,0:T(8,128)(2,1)}), bf16[64,200,128]{2,1,0:T(8,128)(2,1)S(1)}, u32[]{:S(2)}, u32[]{:S(2)}) async-start(bf16[64,200,128]{2,1,0:T(8,128)(2,1)} %shard_map.91), calls=%async_computation | async-start | bytes 6553600 | tf_op jit(solution)/shard_map/all_to_all | solution.py:262
  23.0 0.0 copy-done.12
  23.0 1.8 %pad.9.w1_ref = bf16[384,512]{1,0:T(8,128)(2,1)} pad(bf16[274,512]{1,0:T(8,128)(2,1)} %param.15, bf16[]{:T(256)} %constant.2.clone.1), padding=0_110x0_0 | pad | bytes 673794 | tf_op jit(solution)/shard_map/jit(_pad)/pad | solution.py:265
  24.8 0.0 collective-permute-done
  24.8 2.2 %copy.11 = bf16[274,1024]{0,1:T(8,128)(2,1)} copy(bf16[274,1024]{1,0:T(8,128)(2,1)} %collective-permute-done) | data formatting | bytes 1122304 | tf_op jit(solution)/shard_map/ppermute | solution.py:241
  27.0 0.0 copy-start.2
  27.0 0.0 copy-start.4
  27.0 0.0 copy-start.6
  27.0 1.3 %pad.8.table_ref = bf16[1024,384]{1,0:T(8,128)(2,1)S(1)} pad(bf16[1024,274]{1,0:T(8,128)(2,1)} %bitcast.5, bf16[]{:T(256)} %constant.2.clone.1), padding=0_0x0_110 | pad | bytes 1347586 | tf_op jit(solution)/shard_map/jit(_pad)/pad | solution.py:265
  28.4 0.0 copy-done.2
  28.4 0.1 copy-done.4
  28.4 0.1 copy-done.6
  28.5 1.8 %shard_map.92 = (bf16[1024,384]{1,0:T(8,128)(2,1)S(1)}, bf16[1024,512]{1,0:T(8,128)(2,1)S(1)}, bf16[1024,512]{1,0:T(8,128)(2,1)S(1)}) custom-call(bf16[1024,384]{1,0:T(8,128)(2,1)S(1)} %pad.8.table_ref, bf16[384,512]{1,0:T(8,128)(2,1)S(1)} %copy-done.2, bf16[512,512]{1,0:T(8,128)(2,1)S(1)} %copy-done.4, bf16[512,384]{1,0:T(8,128)(2,1)S(1)} %copy-done.6), custom_call_target="tpu_custom_call" | custom-call | flops 99999997952 | bytes 4000000 | tf_op jit(solution)/shard_map/pallas_call | solution.py:45
  30.3 0.0 copy-start
  30.3 0.9 copy-done
  31.2 0.0 copy-start.8
  31.2 1.0 %copy-done.8 = bf16[1024,512]{1,0:T(8,128)(2,1)} copy-done((bf16[1024,512]{1,0:T(8,128)(2,1)}, bf16[1024,512]{1,0:T(8,128)(2,1)S(1)}, u32[]{:S(2)}) %copy-start.8) | copy-done | bytes 1048600
  32.2 0.0 copy-start.10
  32.2 1.0 %copy-done.10 = bf16[1024,512]{1,0:T(8,128)(2,1)} copy-done((bf16[1024,512]{1,0:T(8,128)(2,1)}, bf16[1024,512]{1,0:T(8,128)(2,1)S(1)}, u32[]{:S(2)}) %copy-start.10) | copy-done | bytes 1048600
  33.2 29.2 %all-to-all-done.arrived_ref = bf16[64,200,128]{2,1,0:T(8,128)(2,1)S(1)} async-done(((bf16[64,200,128]{2,1,0:T(8,128)(2,1)}), bf16[64,200,128]{2,1,0:T(8,128)(2,1)S(1)}, u32[]{:S(2)}, u32[]{:S(2)}) %all-to-all-start) | async-done | bytes 3276832 | tf_op jit(solution)/shard_map/all_to_all | solution.py:262
  62.4 0.0 copy-start.1
  62.4 1.1 %copy-done.1 = bf16[1024,384]{1,0:T(8,128)(2,1)S(1)} copy-done((bf16[1024,384]{1,0:T(8,128)(2,1)S(1)}, bf16[1024,384]{1,0:T(8,128)(2,1)}, u32[]{:S(2)}) %copy-start.1) | copy-done | bytes 786456
  63.6 0.0 copy-start.3
  63.6 0.0 copy-start.5
  63.6 0.0 copy-start.7
  63.6 0.0 copy-start.9
  63.6 0.0 copy-start.11
  63.6 2.9 %shard_map.93 = (bf16[2048,384]{1,0:T(8,128)(2,1)S(1)}, s32[16,128]{1,0:T(8,128)S(1)}) custom-call(bf16[64,200,128]{2,1,0:T(8,128)(2,1)S(1)} %all-to-all-done.arrived_ref, bf16[1024,384]{1,0:T(8,128)(2,1)S(1)} %copy-done.1, f32[1,384]{1,0:T(1,128)S(1)} %reshape.11.sigma_ref), custom_call_target="tpu_custom_call" | custom-call | tf_op jit(solution)/shard_map/pallas_call | solution.py:45
  66.4 0.0 copy-done.3
  66.5 0.0 copy-done.5
  66.5 0.0 copy-done.7
  66.5 0.0 copy-done.9
  66.5 0.0 copy-done.11
  66.5 3.7 %shard_map.94 = (bf16[288,256]{1,0:T(8,128)(2,1)S(1)}, bf16[288,256]{1,0:T(8,128)(2,1)S(1)}, bf16[288,256]{1,0:T(8,128)(2,1)S(1)}, bf16[288,256]{1,0:T(8,128)(2,1)S(1)}) custom-call(s32[16,128]{1,0:T(8,128)S(1)} %get-tuple-element.15.ids_ref, bf16[2048,384]{1,0:T(8,128)(2,1)S(1)} %get-tuple-element.16.departures_ref, bf16[1024,512]{1,0:T(8,128)(2,1)S(1)} %copy-done.9, ...), custom_call_target="tpu_custom_call" | custom-call | flops 8000000000 | bytes 4000000 | tf_op jit(solution)/shard_map/pallas_call | solution.py:45
  70.2 6.1 %collective-permute-start.1 = (bf16[288,256]{1,0:T(8,128)(2,1)S(1)}, bf16[288,256]{1,0:T(8,128)(2,1)S(1)}, u32[]{:S(2)}, u32[]{:S(2)}) collective-permute-start(bf16[288,256]{1,0:T(8,128)(2,1)S(1)} %get-tuple-element.19), channel_id=1, source_target_pairs={{0,2},{1,67},{2,160},{3,193},{4,166},{5,199},{6,4},{7,69},{8,10},{... | collective-permute-start | bytes 442376 | tf_op jit(solution)/shard_map/ppermute | solution.py:290
  76.3 1.6 %collective-permute-start.2 = (bf16[288,256]{1,0:T(8,128)(2,1)S(1)}, bf16[288,256]{1,0:T(8,128)(2,1)S(1)}, u32[]{:S(2)}, u32[]{:S(2)}) collective-permute-start(bf16[288,256]{1,0:T(8,128)(2,1)S(1)} %get-tuple-element.20), channel_id=1, source_target_pairs={{0,1},{1,66},{2,163},{3,192},{4,165},{5,198},{6,7},{7,68},{8,9},{9... | collective-permute-start | bytes 442376 | tf_op jit(solution)/shard_map/ppermute | solution.py:290
  78.0 2.8 %collective-permute-start.3 = (bf16[288,256]{1,0:T(8,128)(2,1)S(1)}, bf16[288,256]{1,0:T(8,128)(2,1)S(1)}, u32[]{:S(2)}, u32[]{:S(2)}) collective-permute-start(bf16[288,256]{1,0:T(8,128)(2,1)S(1)} %get-tuple-element.21), channel_id=1, source_target_pairs={{0,3},{1,64},{2,161},{3,194},{4,167},{5,196},{6,5},{7,70},{8,11},{... | collective-permute-start | bytes 442376 | tf_op jit(solution)/shard_map/ppermute | solution.py:290
  80.8 3.4 %collective-permute-start.4 = (bf16[288,256]{1,0:T(8,128)(2,1)S(1)}, bf16[288,256]{1,0:T(8,128)(2,1)S(1)}, u32[]{:S(2)}, u32[]{:S(2)}) collective-permute-start(bf16[288,256]{1,0:T(8,128)(2,1)S(1)} %get-tuple-element.22), channel_id=1, source_target_pairs={{0,0},{1,65},{2,162},{3,195},{4,164},{5,197},{6,6},{7,71},{8,8},{9... | collective-permute-start | bytes 442376 | tf_op jit(solution)/shard_map/ppermute | solution.py:290
  84.2 0.0 collective-permute-done.1.so_far_ref
  84.2 1.1 %collective-permute-done.2.part_ref = bf16[288,256]{1,0:T(8,128)(2,1)S(1)} collective-permute-done((bf16[288,256]{1,0:T(8,128)(2,1)S(1)}, bf16[288,256]{1,0:T(8,128)(2,1)S(1)}, u32[]{:S(2)}, u32[]{:S(2)}) %collective-permute-start.2) | collective-permute-done | bytes 147488 | tf_op jit(solution)/shard_map/ppermute | solution.py:290
  85.4 2.8 %collective-permute-done.3.part_ref = bf16[288,256]{1,0:T(8,128)(2,1)S(1)} collective-permute-done((bf16[288,256]{1,0:T(8,128)(2,1)S(1)}, bf16[288,256]{1,0:T(8,128)(2,1)S(1)}, u32[]{:S(2)}, u32[]{:S(2)}) %collective-permute-start.3) | collective-permute-done | bytes 147488 | tf_op jit(solution)/shard_map/ppermute | solution.py:290
  88.2 5.0 %collective-permute-done.4.part_ref = bf16[288,256]{1,0:T(8,128)(2,1)S(1)} collective-permute-done((bf16[288,256]{1,0:T(8,128)(2,1)S(1)}, bf16[288,256]{1,0:T(8,128)(2,1)S(1)}, u32[]{:S(2)}, u32[]{:S(2)}) %collective-permute-start.4) | collective-permute-done | bytes 147488 | tf_op jit(solution)/shard_map/ppermute | solution.py:290
  93.2 0.7 shard_map.97
  (3 shorter events, 0.1 us)
Async XLA Ops:
  0.0 24.8 %collective-permute-start = (bf16[274,1024]{1,0:T(8,128)(2,1)}, bf16[274,1024]{1,0:T(8,128)(2,1)}, u32[]{:S(2)}, u32[]{:S(2)}) collective-permute-start(bf16[274,1024]{1,0:T(8,128)(2,1)} %bitcast.8), channel_id=1, source_target_pairs={{0,0},{65,1},{162,2},{195,3},{164,4},{197,5},{6,6},{71,7},{8,8},{7... | collective-permute-start | bytes 1683464 | tf_op jit(solution)/shard_map/ppermute | solution.py:241
  13.5 9.5 %copy-start.12 = (f32[384]{0:T(512)S(1)}, f32[384]{0:T(512)}, u32[]{:S(2)}) copy-start(f32[384]{0:T(512)} %param.13) | copy-start | bytes 4612
  13.5 48.9 %all-to-all-start = ((bf16[64,200,128]{2,1,0:T(8,128)(2,1)}), bf16[64,200,128]{2,1,0:T(8,128)(2,1)S(1)}, u32[]{:S(2)}, u32[]{:S(2)}) async-start(bf16[64,200,128]{2,1,0:T(8,128)(2,1)} %shard_map.91), calls=%async_computation | async-start | bytes 6553600 | tf_op jit(solution)/shard_map/all_to_all | solution.py:262
  27.0 1.3 %copy-start.2 = (bf16[384,512]{1,0:T(8,128)(2,1)S(1)}, bf16[384,512]{1,0:T(8,128)(2,1)}, u32[]{:S(2)}) copy-start(bf16[384,512]{1,0:T(8,128)(2,1)} %pad.9.w1_ref) | copy-start | bytes 1179652
  27.0 1.4 %copy-start.4 = (bf16[512,512]{1,0:T(8,128)(2,1)S(1)}, bf16[512,512]{1,0:T(8,128)(2,1)}, u32[]{:S(2)}) copy-start(bf16[512,512]{1,0:T(8,128)(2,1)} %w2_ref.3) | copy-start | bytes 1572868
  27.0 1.5 %copy-start.6 = (bf16[512,384]{1,0:T(8,128)(2,1)S(1)}, bf16[512,384]{1,0:T(8,128)(2,1)}, u32[]{:S(2)}) copy-start(bf16[512,384]{1,0:T(8,128)(2,1)} %w3_ref.3) | copy-start | bytes 1179652
  30.3 0.9 copy-start
  31.2 1.0 %copy-start.8 = (bf16[1024,512]{1,0:T(8,128)(2,1)}, bf16[1024,512]{1,0:T(8,128)(2,1)S(1)}, u32[]{:S(2)}) copy-start(bf16[1024,512]{1,0:T(8,128)(2,1)S(1)} %get-tuple-element.17.first_ref) | copy-start | bytes 3145732
  32.2 1.0 %copy-start.10 = (bf16[1024,512]{1,0:T(8,128)(2,1)}, bf16[1024,512]{1,0:T(8,128)(2,1)S(1)}, u32[]{:S(2)}) copy-start(bf16[1024,512]{1,0:T(8,128)(2,1)S(1)} %get-tuple-element.18.second_ref) | copy-start | bytes 3145732
  62.4 1.1 %copy-start.1 = (bf16[1024,384]{1,0:T(8,128)(2,1)S(1)}, bf16[1024,384]{1,0:T(8,128)(2,1)}, u32[]{:S(2)}) copy-start(bf16[1024,384]{1,0:T(8,128)(2,1)} %copy-done) | copy-start | bytes 2359300
  63.6 2.9 %copy-start.3 = (bf16[384,512]{1,0:T(8,128)(2,1)S(1)}, bf16[384,512]{1,0:T(8,128)(2,1)}, u32[]{:S(2)}) copy-start(bf16[384,512]{1,0:T(8,128)(2,1)} %pad.9.w1_ref) | copy-start | bytes 1179652
  63.6 2.9 %copy-start.5 = (bf16[512,512]{1,0:T(8,128)(2,1)S(1)}, bf16[512,512]{1,0:T(8,128)(2,1)}, u32[]{:S(2)}) copy-start(bf16[512,512]{1,0:T(8,128)(2,1)} %w2_ref.3) | copy-start | bytes 1572868
  63.6 2.9 %copy-start.7 = (bf16[512,384]{1,0:T(8,128)(2,1)S(1)}, bf16[512,384]{1,0:T(8,128)(2,1)}, u32[]{:S(2)}) copy-start(bf16[512,384]{1,0:T(8,128)(2,1)} %w3_ref.3) | copy-start | bytes 1179652
  63.6 2.9 %copy-start.9 = (bf16[1024,512]{1,0:T(8,128)(2,1)S(1)}, bf16[1024,512]{1,0:T(8,128)(2,1)}, u32[]{:S(2)}) copy-start(bf16[1024,512]{1,0:T(8,128)(2,1)} %copy-done.8) | copy-start | bytes 3145732
  63.6 2.9 %copy-start.11 = (bf16[1024,512]{1,0:T(8,128)(2,1)S(1)}, bf16[1024,512]{1,0:T(8,128)(2,1)}, u32[]{:S(2)}) copy-start(bf16[1024,512]{1,0:T(8,128)(2,1)} %copy-done.10) | copy-start | bytes 3145732
  70.2 13.9 %collective-permute-start.1 = (bf16[288,256]{1,0:T(8,128)(2,1)S(1)}, bf16[288,256]{1,0:T(8,128)(2,1)S(1)}, u32[]{:S(2)}, u32[]{:S(2)}) collective-permute-start(bf16[288,256]{1,0:T(8,128)(2,1)S(1)} %get-tuple-element.19), channel_id=1, source_target_pairs={{0,2},{1,67},{2,160},{3,193},{4,166},{5,199},{6,4},{7,69},{8,10},{... | collective-permute-start | bytes 442376 | tf_op jit(solution)/shard_map/ppermute | solution.py:290
  76.3 9.0 %collective-permute-start.2 = (bf16[288,256]{1,0:T(8,128)(2,1)S(1)}, bf16[288,256]{1,0:T(8,128)(2,1)S(1)}, u32[]{:S(2)}, u32[]{:S(2)}) collective-permute-start(bf16[288,256]{1,0:T(8,128)(2,1)S(1)} %get-tuple-element.20), channel_id=1, source_target_pairs={{0,1},{1,66},{2,163},{3,192},{4,165},{5,198},{6,7},{7,68},{8,9},{9... | collective-permute-start | bytes 442376 | tf_op jit(solution)/shard_map/ppermute | solution.py:290
  78.0 10.2 %collective-permute-start.3 = (bf16[288,256]{1,0:T(8,128)(2,1)S(1)}, bf16[288,256]{1,0:T(8,128)(2,1)S(1)}, u32[]{:S(2)}, u32[]{:S(2)}) collective-permute-start(bf16[288,256]{1,0:T(8,128)(2,1)S(1)} %get-tuple-element.21), channel_id=1, source_target_pairs={{0,3},{1,64},{2,161},{3,194},{4,167},{5,196},{6,5},{7,70},{8,11},{... | collective-permute-start | bytes 442376 | tf_op jit(solution)/shard_map/ppermute | solution.py:290
  80.8 12.4 %collective-permute-start.4 = (bf16[288,256]{1,0:T(8,128)(2,1)S(1)}, bf16[288,256]{1,0:T(8,128)(2,1)S(1)}, u32[]{:S(2)}, u32[]{:S(2)}) collective-permute-start(bf16[288,256]{1,0:T(8,128)(2,1)S(1)} %get-tuple-element.22), channel_id=1, source_target_pairs={{0,0},{1,65},{2,162},{3,195},{4,164},{5,197},{6,6},{7,71},{8,8},{9... | collective-permute-start | bytes 442376 | tf_op jit(solution)/shard_map/ppermute | solution.py:290
where the time goes:
time: 94.6 us; the launch traced here: 93.9 us
  waiting for transfers between devices  38.2 us (40%)
  starting transfers between devices  30.7 us (32%)
  Pallas kernels  15.4 us (16%)
  local copies, waits for them, and re-layouts  9.49 us (10%)
    all_to_all x1, waiting for transfers between devices, on_device(): lax.all_to_all(pushed, GROUP, split_axis=0, concat_axis=0, tiled=True)  29.2 us
    pallas_call x7, Pallas kernels, call(): pl.pallas_call(kernel, out_shape=out, compiler_params=pltpu.CompilerParam...  15.4 us
    ppermute x4, starting transfers between devices, on_device(): lax.ppermute(part, AXES, [(number[p], at_home(p, (p[4] + k) % groups)) fo...  13.9 us
    all_to_all x1, starting transfers between devices, on_device(): lax.all_to_all(pushed, GROUP, split_axis=0, concat_axis=0, tiled=True)  9.48 us
    ppermute x4, waiting for transfers between devices, on_device(): lax.ppermute(part, AXES, [(number[p], at_home(p, (p[4] + k) % groups)) fo...  8.93 us
    ppermute x1, starting transfers between devices, on_device(): lax.ppermute(profiles.T, AXES, [(at_home(p, p[4]), number[p]) for p in ev...  7.3 us
    unnamed x26, local copies, waits for them, and re-layouts  4.19 us
    pad x2, local copies, waits for them, and re-layouts, on_device(): jnp.pad(a, [(0, padded - width) if k == axis else (0, 0) for k in (0, 1)])  3.08 us
  transfers between devices with their start and end apart: 6, of which 4 were waited for; matrix products, arithmetic and copies ran while one was open for 6% of the time, Pallas kernels for 9%

commit v1 on v0

--- a/solution.py
+++ b/solution.py
@@ -148,10 +148,8 @@
     evolved_ref[...] = nn(second, w3_ref[...]).astype(BF16)
 
 
-def departures_kernel(cap, chunk, arrived_ref, evolved_ref, sigma_ref, out_ref, ids_ref):
+def decode_kernel(cap, parts, arrived_ref, ids_ref, column_ref):
     sources = arrived_ref.shape[0]
-    cols, channels = evolved_ref.shape
-    parts = channels // LANES
     digits = arrived_ref[:, 2 * parts * cap :, :].reshape(sources * 8, LANES)
     row = iota((sources, sources * 8), 1) - 8 * iota((sources, sources * 8), 0)
     high = nn(jnp.where(row == 0, 1.0, 0.0).astype(BF16), digits)
@@ -163,13 +161,20 @@
     ).astype(BF16)
     spread = lambda a: nn(gather, jnp.where(mine, a, 0.0).astype(BF16))
     ids_ref[...] = (spread(high) * BASE + spread(low)).astype(jnp.int32)
-    column = (high * BASE + low).T
+    column_ref[...] = (high * BASE + low).T[:cap, :]
+
+
+def departures_kernel(cap, chunk, arrived_ref, column_ref, evolved_ref, sigma_ref, out_ref):
+    sources = arrived_ref.shape[0]
+    cols, channels = evolved_ref.shape
+    parts = channels // LANES
+    column = column_ref[...]
     wide = iota((cap, cols), 1).astype(F32)
     inverse = 1.0 / sigma_ref[...]
     for s in range(0, sources, chunk):
         pick = jnp.concatenate(
             [
-                jnp.where(column[:cap, s + j : s + j + 1] == wide, 1.0, 0.0).astype(BF16)
+                jnp.where(column[:, s + j : s + j + 1] == wide, 1.0, 0.0).astype(BF16)
                 for j in range(chunk)
             ],
             axis=0,
@@ -272,10 +277,17 @@
         cost_estimate=pl.CostEstimate(flops=10**11, bytes_accessed=4 * 10**6, transcendentals=10**6),
     )
 
-    departures, ids = call(
+    ids, column = call(
+        functools.partial(decode_kernel, cap, channels // LANES),
+        (sds((owners * cap // LANES, LANES), jnp.int32), sds((cap, owners), F32)),
+        (arrived,),
+        vmem=32,
+        cost_estimate=pl.CostEstimate(flops=2 * 10**9, bytes_accessed=10**5, transcendentals=0),
+    )
+    departures = call(
         functools.partial(departures_kernel, cap, chunk),
-        (sds((owners * cap, channels), BF16), sds((owners * cap // LANES, LANES), jnp.int32)),
-        (arrived, evolved, sigma.reshape(1, channels)),
+        sds((owners * cap, channels), BF16),
+        (arrived, column, evolved, sigma.reshape(1, channels)),
         vmem=32,
     )
     order = sorted(range(groups), key=lambda k: -min(k, groups - k))

time: 94.6 us -> 94.5 us (level)
    pallas_call x7 -> x8, Pallas kernels: 15.4 us -> 15.6 us  [call(): pl.pallas_call(kernel, out_shape=out, compiler_params=pltpu.CompilerParam...]
where the time goes in v1:
time: 94.5 us; the launch traced here: 93.9 us
  waiting for transfers between devices  38.2 us (40%)
  starting transfers between devices  30.7 us (32%)
  Pallas kernels  15.6 us (17%)
  local copies, waits for them, and re-layouts  9.19 us (10%)
    all_to_all x1, waiting for transfers between devices, on_device(): lax.all_to_all(pushed, GROUP, split_axis=0, concat_axis=0, tiled=True)  29.2 us
    pallas_call x8, Pallas kernels, call(): pl.pallas_call(kernel, out_shape=out, compiler_params=pltpu.CompilerParam...  15.6 us
    ppermute x4, starting transfers between devices, on_device(): lax.ppermute(part, AXES, [(number[p], at_home(p, (p[4] + k) % groups)) fo...  13.9 us
    all_to_all x1, starting transfers between devices, on_device(): lax.all_to_all(pushed, GROUP, split_axis=0, concat_axis=0, tiled=True)  9.48 us
    ppermute x4, waiting for transfers between devices, on_device(): lax.ppermute(part, AXES, [(number[p], at_home(p, (p[4] + k) % groups)) fo...  8.93 us
    ppermute x1, starting transfers between devices, on_device(): lax.ppermute(profiles.T, AXES, [(at_home(p, p[4]), number[p]) for p in ev...  7.3 us
    unnamed x26, local copies, waits for them, and re-layouts  3.89 us
    pad x2, local copies, waits for them, and re-layouts, on_device(): jnp.pad(a, [(0, padded - width) if k == axis else (0, 0) for k in (0, 1)])  3.08 us
  transfers between devices with their start and end apart: 6, of which 4 were waited for; matrix products, arithmetic and copies ran while one was open for 6% of the time, Pallas kernels for 9%

profile of v1, /device:TPU:34, one launch (start us, length us, event | category | flops | bytes accessed | tf_op | source)
XLA Modules:
  0.0 93.9 jit_solution(15682862288718089338)
XLA Ops:
  0.0 7.3 %collective-permute-start = (bf16[274,1024]{1,0:T(8,128)(2,1)}, bf16[274,1024]{1,0:T(8,128)(2,1)}, u32[]{:S(2)}, u32[]{:S(2)}) collective-permute-start(bf16[274,1024]{1,0:T(8,128)(2,1)} %bitcast.8), channel_id=1, source_target_pairs={{0,0},{65,1},{162,2},{195,3},{164,4},{197,5},{6,6},{71,7},{8,8},{7... | collective-permute-start | bytes 1683464 | tf_op jit(solution)/shard_map/ppermute | solution.py:246
  7.3 6.2 %shard_map.91 = bf16[64,200,128]{2,1,0:T(8,128)(2,1)} custom-call(s32[8,128]{1,0:T(8,128)} %bitcast.6, s32[8,128]{1,0:T(8,128)} %bitcast.7, f32[1024,384]{1,0:T(8,128)} %observed_hbm.1, s32[1024,384]{1,0:T(8,128)} %flags_hbm.1), custom_call_target="tpu_custom_call" | custom-call | tf_op jit(solution)/shard_map/pallas_call | solution.py:45
  13.5 0.0 copy-start.12
  13.5 9.5 %all-to-all-start = ((bf16[64,200,128]{2,1,0:T(8,128)(2,1)}), bf16[64,200,128]{2,1,0:T(8,128)(2,1)S(1)}, u32[]{:S(2)}, u32[]{:S(2)}) async-start(bf16[64,200,128]{2,1,0:T(8,128)(2,1)} %shard_map.91), calls=%async_computation | async-start | bytes 6553600 | tf_op jit(solution)/shard_map/all_to_all | solution.py:267
  23.0 0.0 copy-done.12
  23.0 1.8 %pad.9.w1_ref = bf16[384,512]{1,0:T(8,128)(2,1)} pad(bf16[274,512]{1,0:T(8,128)(2,1)} %param.15, bf16[]{:T(256)} %constant.2.clone.1), padding=0_110x0_0 | pad | bytes 673794 | tf_op jit(solution)/shard_map/jit(_pad)/pad | solution.py:270
  24.8 0.0 collective-permute-done
  24.8 2.2 %copy.11 = bf16[274,1024]{0,1:T(8,128)(2,1)} copy(bf16[274,1024]{1,0:T(8,128)(2,1)} %collective-permute-done) | data formatting | bytes 1122304 | tf_op jit(solution)/shard_map/ppermute | solution.py:246
  27.0 0.0 copy-start.2
  27.0 0.0 copy-start.4
  27.0 0.0 copy-start.6
  27.0 1.3 %pad.8.table_ref = bf16[1024,384]{1,0:T(8,128)(2,1)S(1)} pad(bf16[1024,274]{1,0:T(8,128)(2,1)} %bitcast.5, bf16[]{:T(256)} %constant.2.clone.1), padding=0_0x0_110 | pad | bytes 1347586 | tf_op jit(solution)/shard_map/jit(_pad)/pad | solution.py:270
  28.4 0.0 copy-done.2
  28.4 0.1 copy-done.4
  28.4 0.1 copy-done.6
  28.5 1.8 %shard_map.93 = (bf16[1024,384]{1,0:T(8,128)(2,1)S(1)}, bf16[1024,512]{1,0:T(8,128)(2,1)S(1)}, bf16[1024,512]{1,0:T(8,128)(2,1)S(1)}) custom-call(bf16[1024,384]{1,0:T(8,128)(2,1)S(1)} %pad.8.table_ref, bf16[384,512]{1,0:T(8,128)(2,1)S(1)} %copy-done.2, bf16[512,512]{1,0:T(8,128)(2,1)S(1)} %copy-done.4, bf16[512,384]{1,0:T(8,128)(2,1)S(1)} %copy-done.6), custom_call_target="tpu_custom_call" | custom-call | flops 99999997952 | bytes 4000000 | tf_op jit(solution)/shard_map/pallas_call | solution.py:45
  30.3 0.0 copy-start
  30.3 0.9 copy-done
  31.2 0.0 copy-start.8
  31.2 1.0 %copy-done.8 = bf16[1024,512]{1,0:T(8,128)(2,1)} copy-done((bf16[1024,512]{1,0:T(8,128)(2,1)}, bf16[1024,512]{1,0:T(8,128)(2,1)S(1)}, u32[]{:S(2)}) %copy-start.8) | copy-done | bytes 1048600
  32.2 0.0 copy-start.10
  32.2 1.0 %copy-done.10 = bf16[1024,512]{1,0:T(8,128)(2,1)} copy-done((bf16[1024,512]{1,0:T(8,128)(2,1)}, bf16[1024,512]{1,0:T(8,128)(2,1)S(1)}, u32[]{:S(2)}) %copy-start.10) | copy-done | bytes 1048600
  33.2 29.2 %all-to-all-done.arrived_ref = bf16[64,200,128]{2,1,0:T(8,128)(2,1)S(1)} async-done(((bf16[64,200,128]{2,1,0:T(8,128)(2,1)}), bf16[64,200,128]{2,1,0:T(8,128)(2,1)S(1)}, u32[]{:S(2)}, u32[]{:S(2)}) %all-to-all-start) | async-done | bytes 3276832 | tf_op jit(solution)/shard_map/all_to_all | solution.py:267
  62.4 0.0 copy-start.1
  62.4 0.3 shard_map.92
  62.7 0.8 copy-done.1
  63.6 0.0 copy-start.3
  63.6 0.0 copy-start.5
  63.6 0.0 copy-start.7
  63.6 0.0 copy-start.9
  63.6 0.0 copy-start.11
  63.6 2.8 %shard_map.94.departures_ref = bf16[2048,384]{1,0:T(8,128)(2,1)S(1)} custom-call(bf16[64,200,128]{2,1,0:T(8,128)(2,1)S(1)} %all-to-all-done.arrived_ref, f32[32,64]{1,0:T(8,128)S(1)} %get-tuple-element.15.column_ref, bf16[1024,384]{1,0:T(8,128)(2,1)S(1)} %copy-done.1, f32[1,384]{1,0:T(1,128)S(1)} %reshape.11.sigma_ref), custom_call_target="tpu_custom_call" | custom-call | tf_op jit(solution)/shard_map/pallas_call | solution.py:45
  66.4 0.0 copy-done.3
  66.4 0.0 copy-done.5
  66.4 0.0 copy-done.7
  66.4 0.0 copy-done.9
  66.4 0.0 copy-done.11
  66.4 3.8 %shard_map.95 = (bf16[288,256]{1,0:T(8,128)(2,1)S(1)}, bf16[288,256]{1,0:T(8,128)(2,1)S(1)}, bf16[288,256]{1,0:T(8,128)(2,1)S(1)}, bf16[288,256]{1,0:T(8,128)(2,1)S(1)}) custom-call(s32[16,128]{1,0:T(8,128)S(1)} %get-tuple-element.14.ids_ref, bf16[2048,384]{1,0:T(8,128)(2,1)S(1)} %shard_map.94.departures_ref, bf16[1024,512]{1,0:T(8,128)(2,1)S(1)} %copy-done.9, ...), custom_call_target="tpu_custom_call" | custom-call | flops 8000000000 | bytes 4000000 | tf_op jit(solution)/shard_map/pallas_call | solution.py:45
  70.2 6.1 %collective-permute-start.1 = (bf16[288,256]{1,0:T(8,128)(2,1)S(1)}, bf16[288,256]{1,0:T(8,128)(2,1)S(1)}, u32[]{:S(2)}, u32[]{:S(2)}) collective-permute-start(bf16[288,256]{1,0:T(8,128)(2,1)S(1)} %get-tuple-element.19), channel_id=1, source_target_pairs={{0,2},{1,67},{2,160},{3,193},{4,166},{5,199},{6,4},{7,69},{8,10},{... | collective-permute-start | bytes 442376 | tf_op jit(solution)/shard_map/ppermute | solution.py:302
  76.3 1.6 %collective-permute-start.2 = (bf16[288,256]{1,0:T(8,128)(2,1)S(1)}, bf16[288,256]{1,0:T(8,128)(2,1)S(1)}, u32[]{:S(2)}, u32[]{:S(2)}) collective-permute-start(bf16[288,256]{1,0:T(8,128)(2,1)S(1)} %get-tuple-element.20), channel_id=1, source_target_pairs={{0,1},{1,66},{2,163},{3,192},{4,165},{5,198},{6,7},{7,68},{8,9},{9... | collective-permute-start | bytes 442376 | tf_op jit(solution)/shard_map/ppermute | solution.py:302
  77.9 2.8 %collective-permute-start.3 = (bf16[288,256]{1,0:T(8,128)(2,1)S(1)}, bf16[288,256]{1,0:T(8,128)(2,1)S(1)}, u32[]{:S(2)}, u32[]{:S(2)}) collective-permute-start(bf16[288,256]{1,0:T(8,128)(2,1)S(1)} %get-tuple-element.21), channel_id=1, source_target_pairs={{0,3},{1,64},{2,161},{3,194},{4,167},{5,196},{6,5},{7,70},{8,11},{... | collective-permute-start | bytes 442376 | tf_op jit(solution)/shard_map/ppermute | solution.py:302
  80.7 3.4 %collective-permute-start.4 = (bf16[288,256]{1,0:T(8,128)(2,1)S(1)}, bf16[288,256]{1,0:T(8,128)(2,1)S(1)}, u32[]{:S(2)}, u32[]{:S(2)}) collective-permute-start(bf16[288,256]{1,0:T(8,128)(2,1)S(1)} %get-tuple-element.22), channel_id=1, source_target_pairs={{0,0},{1,65},{2,162},{3,195},{4,164},{5,197},{6,6},{7,71},{8,8},{9... | collective-permute-start | bytes 442376 | tf_op jit(solution)/shard_map/ppermute | solution.py:302
  84.1 0.0 collective-permute-done.1.so_far_ref
  84.1 1.1 %collective-permute-done.2.part_ref = bf16[288,256]{1,0:T(8,128)(2,1)S(1)} collective-permute-done((bf16[288,256]{1,0:T(8,128)(2,1)S(1)}, bf16[288,256]{1,0:T(8,128)(2,1)S(1)}, u32[]{:S(2)}, u32[]{:S(2)}) %collective-permute-start.2) | collective-permute-done | bytes 147488 | tf_op jit(solution)/shard_map/ppermute | solution.py:302
  85.3 2.8 %collective-permute-done.3.part_ref = bf16[288,256]{1,0:T(8,128)(2,1)S(1)} collective-permute-done((bf16[288,256]{1,0:T(8,128)(2,1)S(1)}, bf16[288,256]{1,0:T(8,128)(2,1)S(1)}, u32[]{:S(2)}, u32[]{:S(2)}) %collective-permute-start.3) | collective-permute-done | bytes 147488 | tf_op jit(solution)/shard_map/ppermute | solution.py:302
  88.1 5.0 %collective-permute-done.4.part_ref = bf16[288,256]{1,0:T(8,128)(2,1)S(1)} collective-permute-done((bf16[288,256]{1,0:T(8,128)(2,1)S(1)}, bf16[288,256]{1,0:T(8,128)(2,1)S(1)}, u32[]{:S(2)}, u32[]{:S(2)}) %collective-permute-start.4) | collective-permute-done | bytes 147488 | tf_op jit(solution)/shard_map/ppermute | solution.py:302
  93.1 0.7 shard_map.98
  (3 shorter events, 0.1 us)
Async XLA Ops:
  0.0 24.8 %collective-permute-start = (bf16[274,1024]{1,0:T(8,128)(2,1)}, bf16[274,1024]{1,0:T(8,128)(2,1)}, u32[]{:S(2)}, u32[]{:S(2)}) collective-permute-start(bf16[274,1024]{1,0:T(8,128)(2,1)} %bitcast.8), channel_id=1, source_target_pairs={{0,0},{65,1},{162,2},{195,3},{164,4},{197,5},{6,6},{71,7},{8,8},{7... | collective-permute-start | bytes 1683464 | tf_op jit(solution)/shard_map/ppermute | solution.py:246
  13.5 9.5 %copy-start.12 = (f32[384]{0:T(512)S(1)}, f32[384]{0:T(512)}, u32[]{:S(2)}) copy-start(f32[384]{0:T(512)} %param.13) | copy-start | bytes 4612
  13.5 48.9 %all-to-all-start = ((bf16[64,200,128]{2,1,0:T(8,128)(2,1)}), bf16[64,200,128]{2,1,0:T(8,128)(2,1)S(1)}, u32[]{:S(2)}, u32[]{:S(2)}) async-start(bf16[64,200,128]{2,1,0:T(8,128)(2,1)} %shard_map.91), calls=%async_computation | async-start | bytes 6553600 | tf_op jit(solution)/shard_map/all_to_all | solution.py:267
  27.0 1.3 %copy-start.2 = (bf16[384,512]{1,0:T(8,128)(2,1)S(1)}, bf16[384,512]{1,0:T(8,128)(2,1)}, u32[]{:S(2)}) copy-start(bf16[384,512]{1,0:T(8,128)(2,1)} %pad.9.w1_ref) | copy-start | bytes 1179652
  27.0 1.4 %copy-start.4 = (bf16[512,512]{1,0:T(8,128)(2,1)S(1)}, bf16[512,512]{1,0:T(8,128)(2,1)}, u32[]{:S(2)}) copy-start(bf16[512,512]{1,0:T(8,128)(2,1)} %w2_ref.3) | copy-start | bytes 1572868
  27.0 1.5 %copy-start.6 = (bf16[512,384]{1,0:T(8,128)(2,1)S(1)}, bf16[512,384]{1,0:T(8,128)(2,1)}, u32[]{:S(2)}) copy-start(bf16[512,384]{1,0:T(8,128)(2,1)} %w3_ref.3) | copy-start | bytes 1179652
  30.3 0.9 copy-start
  31.2 1.0 %copy-start.8 = (bf16[1024,512]{1,0:T(8,128)(2,1)}, bf16[1024,512]{1,0:T(8,128)(2,1)S(1)}, u32[]{:S(2)}) copy-start(bf16[1024,512]{1,0:T(8,128)(2,1)S(1)} %get-tuple-element.17.first_ref) | copy-start | bytes 3145732
  32.2 1.0 %copy-start.10 = (bf16[1024,512]{1,0:T(8,128)(2,1)}, bf16[1024,512]{1,0:T(8,128)(2,1)S(1)}, u32[]{:S(2)}) copy-start(bf16[1024,512]{1,0:T(8,128)(2,1)S(1)} %get-tuple-element.18.second_ref) | copy-start | bytes 3145732
  62.4 1.1 %copy-start.1 = (bf16[1024,384]{1,0:T(8,128)(2,1)S(1)}, bf16[1024,384]{1,0:T(8,128)(2,1)}, u32[]{:S(2)}) copy-start(bf16[1024,384]{1,0:T(8,128)(2,1)} %copy-done) | copy-start | bytes 2359300
  63.6 2.8 %copy-start.3 = (bf16[384,512]{1,0:T(8,128)(2,1)S(1)}, bf16[384,512]{1,0:T(8,128)(2,1)}, u32[]{:S(2)}) copy-start(bf16[384,512]{1,0:T(8,128)(2,1)} %pad.9.w1_ref) | copy-start | bytes 1179652
  63.6 2.8 %copy-start.5 = (bf16[512,512]{1,0:T(8,128)(2,1)S(1)}, bf16[512,512]{1,0:T(8,128)(2,1)}, u32[]{:S(2)}) copy-start(bf16[512,512]{1,0:T(8,128)(2,1)} %w2_ref.3) | copy-start | bytes 1572868
  63.6 2.8 %copy-start.7 = (bf16[512,384]{1,0:T(8,128)(2,1)S(1)}, bf16[512,384]{1,0:T(8,128)(2,1)}, u32[]{:S(2)}) copy-start(bf16[512,384]{1,0:T(8,128)(2,1)} %w3_ref.3) | copy-start | bytes 1179652
  63.6 2.8 %copy-start.9 = (bf16[1024,512]{1,0:T(8,128)(2,1)S(1)}, bf16[1024,512]{1,0:T(8,128)(2,1)}, u32[]{:S(2)}) copy-start(bf16[1024,512]{1,0:T(8,128)(2,1)} %copy-done.8) | copy-start | bytes 3145732
  63.6 2.8 %copy-start.11 = (bf16[1024,512]{1,0:T(8,128)(2,1)S(1)}, bf16[1024,512]{1,0:T(8,128)(2,1)}, u32[]{:S(2)}) copy-start(bf16[1024,512]{1,0:T(8,128)(2,1)} %copy-done.10) | copy-start | bytes 3145732
  70.2 13.9 %collective-permute-start.1 = (bf16[288,256]{1,0:T(8,128)(2,1)S(1)}, bf16[288,256]{1,0:T(8,128)(2,1)S(1)}, u32[]{:S(2)}, u32[]{:S(2)}) collective-permute-start(bf16[288,256]{1,0:T(8,128)(2,1)S(1)} %get-tuple-element.19), channel_id=1, source_target_pairs={{0,2},{1,67},{2,160},{3,193},{4,166},{5,199},{6,4},{7,69},{8,10},{... | collective-permute-start | bytes 442376 | tf_op jit(solution)/shard_map/ppermute | solution.py:302
  76.3 9.0 %collective-permute-start.2 = (bf16[288,256]{1,0:T(8,128)(2,1)S(1)}, bf16[288,256]{1,0:T(8,128)(2,1)S(1)}, u32[]{:S(2)}, u32[]{:S(2)}) collective-permute-start(bf16[288,256]{1,0:T(8,128)(2,1)S(1)} %get-tuple-element.20), channel_id=1, source_target_pairs={{0,1},{1,66},{2,163},{3,192},{4,165},{5,198},{6,7},{7,68},{8,9},{9... | collective-permute-start | bytes 442376 | tf_op jit(solution)/shard_map/ppermute | solution.py:302
  77.9 10.2 %collective-permute-start.3 = (bf16[288,256]{1,0:T(8,128)(2,1)S(1)}, bf16[288,256]{1,0:T(8,128)(2,1)S(1)}, u32[]{:S(2)}, u32[]{:S(2)}) collective-permute-start(bf16[288,256]{1,0:T(8,128)(2,1)S(1)} %get-tuple-element.21), channel_id=1, source_target_pairs={{0,3},{1,64},{2,161},{3,194},{4,167},{5,196},{6,5},{7,70},{8,11},{... | collective-permute-start | bytes 442376 | tf_op jit(solution)/shard_map/ppermute | solution.py:302
  80.7 12.4 %collective-permute-start.4 = (bf16[288,256]{1,0:T(8,128)(2,1)S(1)}, bf16[288,256]{1,0:T(8,128)(2,1)S(1)}, u32[]{:S(2)}, u32[]{:S(2)}) collective-permute-start(bf16[288,256]{1,0:T(8,128)(2,1)S(1)} %get-tuple-element.22), channel_id=1, source_target_pairs={{0,0},{1,65},{2,162},{3,195},{4,164},{5,197},{6,6},{7,71},{8,8},{9... | collective-permute-start | bytes 442376 | tf_op jit(solution)/shard_map/ppermute | solution.py:302

commit v2 on v1

--- a/solution.py
+++ b/solution.py
@@ -148,7 +148,13 @@
     evolved_ref[...] = nn(second, w3_ref[...]).astype(BF16)
 
 
-def decode_kernel(cap, parts, arrived_ref, ids_ref, column_ref):
+def one_hot(cap, column, sources, cols):
+    wide = iota((cap, cols), 1).astype(F32)
+    picks = [jnp.where(column[:, s : s + 1] == wide, 1.0, 0.0).astype(BF16) for s in sources]
+    return jnp.concatenate(picks, axis=0)
+
+
+def decode_kernel(cap, chunk, parts, arrived_ref, ids_ref, column_ref, pick_ref):
     sources = arrived_ref.shape[0]
     digits = arrived_ref[:, 2 * parts * cap :, :].reshape(sources * 8, LANES)
     row = iota((sources, sources * 8), 1) - 8 * iota((sources, sources * 8), 0)
@@ -161,24 +167,26 @@
     ).astype(BF16)
     spread = lambda a: nn(gather, jnp.where(mine, a, 0.0).astype(BF16))
     ids_ref[...] = (spread(high) * BASE + spread(low)).astype(jnp.int32)
-    column_ref[...] = (high * BASE + low).T[:cap, :]
-
-
-def departures_kernel(cap, chunk, arrived_ref, column_ref, evolved_ref, sigma_ref, out_ref):
+    column = (high * BASE + low).T[:cap, :]
+    column_ref[...] = column
+    count, cols = pick_ref.shape
+    for s in range(0, count // cap, chunk):
+        pick_ref[s * cap : (s + chunk) * cap, :] = one_hot(cap, column, range(s, s + chunk), cols)
+
+
+def departures_kernel(
+    cap, chunk, arrived_ref, column_ref, pick_ref, evolved_ref, sigma_ref, out_ref
+):
     sources = arrived_ref.shape[0]
     cols, channels = evolved_ref.shape
     parts = channels // LANES
     column = column_ref[...]
-    wide = iota((cap, cols), 1).astype(F32)
     inverse = 1.0 / sigma_ref[...]
     for s in range(0, sources, chunk):
-        pick = jnp.concatenate(
-            [
-                jnp.where(column[:, s + j : s + j + 1] == wide, 1.0, 0.0).astype(BF16)
-                for j in range(chunk)
-            ],
-            axis=0,
-        )
+        if s * cap < pick_ref.shape[0]:
+            pick = pick_ref[s * cap : (s + chunk) * cap, :]
+        else:
+            pick = one_hot(cap, column, range(s, s + chunk), cols)
         evolved = nn(pick, evolved_ref[...])
         for j in range(parts):
             lanes = slice(j * LANES, (j + 1) * LANES)
@@ -277,9 +285,13 @@
         cost_estimate=pl.CostEstimate(flops=10**11, bytes_accessed=4 * 10**6, transcendentals=10**6),
     )
 
-    ids, column = call(
-        functools.partial(decode_kernel, cap, channels // LANES),
-        (sds((owners * cap // LANES, LANES), jnp.int32), sds((cap, owners), F32)),
+    ids, column, pick = call(
+        functools.partial(decode_kernel, cap, chunk, channels // LANES),
+        (
+            sds((owners * cap // LANES, LANES), jnp.int32),
+            sds((cap, owners), F32),
+            sds((2 * chunk * cap, cols), BF16),
+        ),
         (arrived,),
         vmem=32,
         cost_estimate=pl.CostEstimate(flops=2 * 10**9, bytes_accessed=10**5, transcendentals=0),
@@ -287,7 +299,7 @@
     departures = call(
         functools.partial(departures_kernel, cap, chunk),
         sds((owners * cap, channels), BF16),
-        (arrived, column, evolved, sigma.reshape(1, channels)),
+        (arrived, column, pick, evolved, sigma.reshape(1, channels)),
         vmem=32,
     )
     order = sorted(range(groups), key=lambda k: -min(k, groups - k))

time: 94.5 us -> 94.6 us (level)
  waiting for transfers between devices: 38.2 us -> 35.4 us
  local copies, waits for them, and re-layouts: 9.19 us -> 11.6 us
    all_to_all x1, waiting for transfers between devices: 29.2 us -> 26.5 us  [on_device(): lax.all_to_all(pushed, GROUP, split_axis=0, concat_axis=0, tiled=True)]
    unnamed x26, local copies, waits for them, and re-layouts: 3.89 us -> 6.39 us
where the time goes in v2:
time: 94.6 us; the launch traced here: 93.8 us
  waiting for transfers between devices  35.4 us (37%)
  starting transfers between devices  30.7 us (32%)
  Pallas kernels  15.9 us (17%)
  local copies, waits for them, and re-layouts  11.6 us (12%)
    all_to_all x1, waiting for transfers between devices, on_device(): lax.all_to_all(pushed, GROUP, split_axis=0, concat_axis=0, tiled=True)  26.5 us
    pallas_call x8, Pallas kernels, call(): pl.pallas_call(kernel, out_shape=out, compiler_params=pltpu.CompilerParam...  15.9 us
    ppermute x4, starting transfers between devices, on_device(): lax.ppermute(part, AXES, [(number[p], at_home(p, (p[4] + k) % groups)) fo...  13.9 us
    all_to_all x1, starting transfers between devices, on_device(): lax.all_to_all(pushed, GROUP, split_axis=0, concat_axis=0, tiled=True)  9.48 us
    ppermute x4, waiting for transfers between devices, on_device(): lax.ppermute(part, AXES, [(number[p], at_home(p, (p[4] + k) % groups)) fo...  8.93 us
    ppermute x1, starting transfers between devices, on_device(): lax.ppermute(profiles.T, AXES, [(at_home(p, p[4]), number[p]) for p in ev...  7.3 us
    unnamed x26, local copies, waits for them, and re-layouts  6.39 us
    pad x2, local copies, waits for them, and re-layouts, on_device(): jnp.pad(a, [(0, padded - width) if k == axis else (0, 0) for k in (0, 1)])  2.98 us
  transfers between devices with their start and end apart: 6, of which 4 were waited for; matrix products, arithmetic and copies ran while one was open for 6% of the time, Pallas kernels for 9%

profile of v2, /device:TPU:34, one launch (start us, length us, event | category | flops | bytes accessed | tf_op | source)
XLA Modules:
  0.0 93.8 jit_solution(9512603896523352962)
XLA Ops:
  0.0 7.3 %collective-permute-start = (bf16[274,1024]{1,0:T(8,128)(2,1)}, bf16[274,1024]{1,0:T(8,128)(2,1)}, u32[]{:S(2)}, u32[]{:S(2)}) collective-permute-start(bf16[274,1024]{1,0:T(8,128)(2,1)} %bitcast.8), channel_id=1, source_target_pairs={{0,0},{65,1},{162,2},{195,3},{164,4},{197,5},{6,6},{71,7},{8,8},{7... | collective-permute-start | bytes 1683464 | tf_op jit(solution)/shard_map/ppermute | solution.py:254
  7.3 6.2 %shard_map.91 = bf16[64,200,128]{2,1,0:T(8,128)(2,1)} custom-call(s32[8,128]{1,0:T(8,128)} %bitcast.6, s32[8,128]{1,0:T(8,128)} %bitcast.7, f32[1024,384]{1,0:T(8,128)} %observed_hbm.1, s32[1024,384]{1,0:T(8,128)} %flags_hbm.1), custom_call_target="tpu_custom_call" | custom-call | tf_op jit(solution)/shard_map/pallas_call | solution.py:45
  13.5 0.0 copy-start.12
  13.5 9.5 %all-to-all-start = ((bf16[64,200,128]{2,1,0:T(8,128)(2,1)}), bf16[64,200,128]{2,1,0:T(8,128)(2,1)S(1)}, u32[]{:S(2)}, u32[]{:S(2)}) async-start(bf16[64,200,128]{2,1,0:T(8,128)(2,1)} %shard_map.91), calls=%async_computation | async-start | bytes 6553600 | tf_op jit(solution)/shard_map/all_to_all | solution.py:275
  23.0 0.0 copy-done.12
  23.0 1.8 %pad.9.w1_ref = bf16[384,512]{1,0:T(8,128)(2,1)} pad(bf16[274,512]{1,0:T(8,128)(2,1)} %param.15, bf16[]{:T(256)} %constant.2.clone.1), padding=0_110x0_0 | pad | bytes 673794 | tf_op jit(solution)/shard_map/jit(_pad)/pad | solution.py:278
  24.8 0.0 collective-permute-done
  24.8 2.2 %copy.11 = bf16[274,1024]{0,1:T(8,128)(2,1)} copy(bf16[274,1024]{1,0:T(8,128)(2,1)} %collective-permute-done) | data formatting | bytes 1122304 | tf_op jit(solution)/shard_map/ppermute | solution.py:254
  27.0 1.2 %pad.8.table_ref = bf16[1024,384]{1,0:T(8,128)(2,1)S(1)} pad(bf16[1024,274]{1,0:T(8,128)(2,1)} %bitcast.5, bf16[]{:T(256)} %constant.2.clone.1), padding=0_0x0_110 | pad | bytes 1347586 | tf_op jit(solution)/shard_map/jit(_pad)/pad | solution.py:278
  28.2 0.0 copy-start.2
  28.3 1.0 %copy-done.2 = bf16[384,512]{1,0:T(8,128)(2,1)S(1)} copy-done((bf16[384,512]{1,0:T(8,128)(2,1)S(1)}, bf16[384,512]{1,0:T(8,128)(2,1)}, u32[]{:S(2)}) %copy-start.2) | copy-done | bytes 393240
  29.2 0.0 copy-start.4
  29.2 1.0 %copy-done.4 = bf16[512,512]{1,0:T(8,128)(2,1)S(1)} copy-done((bf16[512,512]{1,0:T(8,128)(2,1)S(1)}, bf16[512,512]{1,0:T(8,128)(2,1)}, u32[]{:S(2)}) %copy-start.4) | copy-done | bytes 524312
  30.3 0.0 copy-start.6
  30.3 1.0 %copy-done.6 = bf16[512,384]{1,0:T(8,128)(2,1)S(1)} copy-done((bf16[512,384]{1,0:T(8,128)(2,1)S(1)}, bf16[512,384]{1,0:T(8,128)(2,1)}, u32[]{:S(2)}) %copy-start.6) | copy-done | bytes 393240
  31.3 1.8 %shard_map.93 = (bf16[1024,384]{1,0:T(8,128)(2,1)S(1)}, bf16[1024,512]{1,0:T(8,128)(2,1)S(1)}, bf16[1024,512]{1,0:T(8,128)(2,1)S(1)}) custom-call(bf16[1024,384]{1,0:T(8,128)(2,1)S(1)} %pad.8.table_ref, bf16[384,512]{1,0:T(8,128)(2,1)S(1)} %copy-done.2, bf16[512,512]{1,0:T(8,128)(2,1)S(1)} %copy-done.4, bf16[512,384]{1,0:T(8,128)(2,1)S(1)} %copy-done.6), custom_call_target="tpu_custom_call" | custom-call | flops 99999997952 | bytes 4000000 | tf_op jit(solution)/shard_map/pallas_call | solution.py:45
  33.1 0.0 copy-start
  33.1 0.9 copy-done
  34.0 0.0 copy-start.8
  34.0 1.0 %copy-done.8 = bf16[1024,512]{1,0:T(8,128)(2,1)} copy-done((bf16[1024,512]{1,0:T(8,128)(2,1)}, bf16[1024,512]{1,0:T(8,128)(2,1)S(1)}, u32[]{:S(2)}) %copy-start.8) | copy-done | bytes 1048600
  34.9 0.0 copy-start.10
  34.9 1.0 %copy-done.10 = bf16[1024,512]{1,0:T(8,128)(2,1)} copy-done((bf16[1024,512]{1,0:T(8,128)(2,1)}, bf16[1024,512]{1,0:T(8,128)(2,1)S(1)}, u32[]{:S(2)}) %copy-start.10) | copy-done | bytes 1048600
  35.9 26.5 %all-to-all-done.arrived_ref = bf16[64,200,128]{2,1,0:T(8,128)(2,1)S(1)} async-done(((bf16[64,200,128]{2,1,0:T(8,128)(2,1)}), bf16[64,200,128]{2,1,0:T(8,128)(2,1)S(1)}, u32[]{:S(2)}, u32[]{:S(2)}) %all-to-all-start) | async-done | bytes 3276832 | tf_op jit(solution)/shard_map/all_to_all | solution.py:275
  62.4 0.0 copy-start.1
  62.4 0.6 shard_map.92
  63.1 0.5 copy-done.1
  63.6 0.0 copy-start.3
  63.6 0.0 copy-start.5
  63.6 0.0 copy-start.7
  63.6 0.0 copy-start.9
  63.6 0.0 copy-start.11
  63.6 2.7 %shard_map.94.departures_ref = bf16[2048,384]{1,0:T(8,128)(2,1)S(1)} custom-call(bf16[64,200,128]{2,1,0:T(8,128)(2,1)S(1)} %all-to-all-done.arrived_ref, f32[32,64]{1,0:T(8,128)S(1)} %get-tuple-element.16.column_ref, bf16[1024,1024]{1,0:T(8,128)(2,1)S(1)} %get-tuple-element.17.pick_ref, bf16[1024,384]{1,0:T(8,128)(2,1)S(1)} %copy-done.1, ...), custom_call_target="tpu_custom_call" | custom-call | tf_op jit(solution)/shard_map/pallas_call | solution.py:45
  66.3 0.0 copy-done.3
  66.3 0.0 copy-done.5
  66.3 0.0 copy-done.7
  66.3 0.0 copy-done.9
  66.3 0.0 copy-done.11
  66.4 3.8 %shard_map.95 = (bf16[288,256]{1,0:T(8,128)(2,1)S(1)}, bf16[288,256]{1,0:T(8,128)(2,1)S(1)}, bf16[288,256]{1,0:T(8,128)(2,1)S(1)}, bf16[288,256]{1,0:T(8,128)(2,1)S(1)}) custom-call(s32[16,128]{1,0:T(8,128)S(1)} %get-tuple-element.15.ids_ref, bf16[2048,384]{1,0:T(8,128)(2,1)S(1)} %shard_map.94.departures_ref, bf16[1024,512]{1,0:T(8,128)(2,1)S(1)} %copy-done.9, ...), custom_call_target="tpu_custom_call" | custom-call | flops 8000000000 | bytes 4000000 | tf_op jit(solution)/shard_map/pallas_call | solution.py:45
  70.1 6.1 %collective-permute-start.1 = (bf16[288,256]{1,0:T(8,128)(2,1)S(1)}, bf16[288,256]{1,0:T(8,128)(2,1)S(1)}, u32[]{:S(2)}, u32[]{:S(2)}) collective-permute-start(bf16[288,256]{1,0:T(8,128)(2,1)S(1)} %get-tuple-element.21), channel_id=1, source_target_pairs={{0,2},{1,67},{2,160},{3,193},{4,166},{5,199},{6,4},{7,69},{8,10},{... | collective-permute-start | bytes 442376 | tf_op jit(solution)/shard_map/ppermute | solution.py:314
  76.2 1.6 %collective-permute-start.2 = (bf16[288,256]{1,0:T(8,128)(2,1)S(1)}, bf16[288,256]{1,0:T(8,128)(2,1)S(1)}, u32[]{:S(2)}, u32[]{:S(2)}) collective-permute-start(bf16[288,256]{1,0:T(8,128)(2,1)S(1)} %get-tuple-element.22), channel_id=1, source_target_pairs={{0,1},{1,66},{2,163},{3,192},{4,165},{5,198},{6,7},{7,68},{8,9},{9... | collective-permute-start | bytes 442376 | tf_op jit(solution)/shard_map/ppermute | solution.py:314
  77.8 2.8 %collective-permute-start.3 = (bf16[288,256]{1,0:T(8,128)(2,1)S(1)}, bf16[288,256]{1,0:T(8,128)(2,1)S(1)}, u32[]{:S(2)}, u32[]{:S(2)}) collective-permute-start(bf16[288,256]{1,0:T(8,128)(2,1)S(1)} %get-tuple-element.23), channel_id=1, source_target_pairs={{0,3},{1,64},{2,161},{3,194},{4,167},{5,196},{6,5},{7,70},{8,11},{... | collective-permute-start | bytes 442376 | tf_op jit(solution)/shard_map/ppermute | solution.py:314
  80.7 3.4 %collective-permute-start.4 = (bf16[288,256]{1,0:T(8,128)(2,1)S(1)}, bf16[288,256]{1,0:T(8,128)(2,1)S(1)}, u32[]{:S(2)}, u32[]{:S(2)}) collective-permute-start(bf16[288,256]{1,0:T(8,128)(2,1)S(1)} %get-tuple-element.24), channel_id=1, source_target_pairs={{0,0},{1,65},{2,162},{3,195},{4,164},{5,197},{6,6},{7,71},{8,8},{9... | collective-permute-start | bytes 442376 | tf_op jit(solution)/shard_map/ppermute | solution.py:314
  84.1 0.0 collective-permute-done.1.so_far_ref
  84.1 1.1 %collective-permute-done.2.part_ref = bf16[288,256]{1,0:T(8,128)(2,1)S(1)} collective-permute-done((bf16[288,256]{1,0:T(8,128)(2,1)S(1)}, bf16[288,256]{1,0:T(8,128)(2,1)S(1)}, u32[]{:S(2)}, u32[]{:S(2)}) %collective-permute-start.2) | collective-permute-done | bytes 147488 | tf_op jit(solution)/shard_map/ppermute | solution.py:314
  85.2 2.8 %collective-permute-done.3.part_ref = bf16[288,256]{1,0:T(8,128)(2,1)S(1)} collective-permute-done((bf16[288,256]{1,0:T(8,128)(2,1)S(1)}, bf16[288,256]{1,0:T(8,128)(2,1)S(1)}, u32[]{:S(2)}, u32[]{:S(2)}) %collective-permute-start.3) | collective-permute-done | bytes 147488 | tf_op jit(solution)/shard_map/ppermute | solution.py:314
  88.0 5.0 %collective-permute-done.4.part_ref = bf16[288,256]{1,0:T(8,128)(2,1)S(1)} collective-permute-done((bf16[288,256]{1,0:T(8,128)(2,1)S(1)}, bf16[288,256]{1,0:T(8,128)(2,1)S(1)}, u32[]{:S(2)}, u32[]{:S(2)}) %collective-permute-start.4) | collective-permute-done | bytes 147488 | tf_op jit(solution)/shard_map/ppermute | solution.py:314
  93.1 0.7 shard_map.98
  (3 shorter events, 0.1 us)
Async XLA Ops:
  0.0 24.8 %collective-permute-start = (bf16[274,1024]{1,0:T(8,128)(2,1)}, bf16[274,1024]{1,0:T(8,128)(2,1)}, u32[]{:S(2)}, u32[]{:S(2)}) collective-permute-start(bf16[274,1024]{1,0:T(8,128)(2,1)} %bitcast.8), channel_id=1, source_target_pairs={{0,0},{65,1},{162,2},{195,3},{164,4},{197,5},{6,6},{71,7},{8,8},{7... | collective-permute-start | bytes 1683464 | tf_op jit(solution)/shard_map/ppermute | solution.py:254
  13.5 9.5 %copy-start.12 = (f32[384]{0:T(512)S(1)}, f32[384]{0:T(512)}, u32[]{:S(2)}) copy-start(f32[384]{0:T(512)} %param.13) | copy-start | bytes 4612
  13.5 48.9 %all-to-all-start = ((bf16[64,200,128]{2,1,0:T(8,128)(2,1)}), bf16[64,200,128]{2,1,0:T(8,128)(2,1)S(1)}, u32[]{:S(2)}, u32[]{:S(2)}) async-start(bf16[64,200,128]{2,1,0:T(8,128)(2,1)} %shard_map.91), calls=%async_computation | async-start | bytes 6553600 | tf_op jit(solution)/shard_map/all_to_all | solution.py:275
  28.2 1.0 %copy-start.2 = (bf16[384,512]{1,0:T(8,128)(2,1)S(1)}, bf16[384,512]{1,0:T(8,128)(2,1)}, u32[]{:S(2)}) copy-start(bf16[384,512]{1,0:T(8,128)(2,1)} %pad.9.w1_ref) | copy-start | bytes 1179652
  29.2 1.0 %copy-start.4 = (bf16[512,512]{1,0:T(8,128)(2,1)S(1)}, bf16[512,512]{1,0:T(8,128)(2,1)}, u32[]{:S(2)}) copy-start(bf16[512,512]{1,0:T(8,128)(2,1)} %w2_ref.3) | copy-start | bytes 1572868
  30.3 1.0 %copy-start.6 = (bf16[512,384]{1,0:T(8,128)(2,1)S(1)}, bf16[512,384]{1,0:T(8,128)(2,1)}, u32[]{:S(2)}) copy-start(bf16[512,384]{1,0:T(8,128)(2,1)} %w3_ref.3) | copy-start | bytes 1179652
  33.1 0.9 copy-start
  34.0 1.0 %copy-start.8 = (bf16[1024,512]{1,0:T(8,128)(2,1)}, bf16[1024,512]{1,0:T(8,128)(2,1)S(1)}, u32[]{:S(2)}) copy-start(bf16[1024,512]{1,0:T(8,128)(2,1)S(1)} %get-tuple-element.19.first_ref) | copy-start | bytes 3145732
  34.9 1.0 %copy-start.10 = (bf16[1024,512]{1,0:T(8,128)(2,1)}, bf16[1024,512]{1,0:T(8,128)(2,1)S(1)}, u32[]{:S(2)}) copy-start(bf16[1024,512]{1,0:T(8,128)(2,1)S(1)} %get-tuple-element.20.second_ref) | copy-start | bytes 3145732
  62.4 1.1 %copy-start.1 = (bf16[1024,384]{1,0:T(8,128)(2,1)S(1)}, bf16[1024,384]{1,0:T(8,128)(2,1)}, u32[]{:S(2)}) copy-start(bf16[1024,384]{1,0:T(8,128)(2,1)} %copy-done) | copy-start | bytes 2359300
  63.6 2.7 %copy-start.3 = (bf16[384,512]{1,0:T(8,128)(2,1)S(1)}, bf16[384,512]{1,0:T(8,128)(2,1)}, u32[]{:S(2)}) copy-start(bf16[384,512]{1,0:T(8,128)(2,1)} %pad.9.w1_ref) | copy-start | bytes 1179652
  63.6 2.8 %copy-start.5 = (bf16[512,512]{1,0:T(8,128)(2,1)S(1)}, bf16[512,512]{1,0:T(8,128)(2,1)}, u32[]{:S(2)}) copy-start(bf16[512,512]{1,0:T(8,128)(2,1)} %w2_ref.3) | copy-start | bytes 1572868
  63.6 2.8 %copy-start.7 = (bf16[512,384]{1,0:T(8,128)(2,1)S(1)}, bf16[512,384]{1,0:T(8,128)(2,1)}, u32[]{:S(2)}) copy-start(bf16[512,384]{1,0:T(8,128)(2,1)} %w3_ref.3) | copy-start | bytes 1179652
  63.6 2.8 %copy-start.9 = (bf16[1024,512]{1,0:T(8,128)(2,1)S(1)}, bf16[1024,512]{1,0:T(8,128)(2,1)}, u32[]{:S(2)}) copy-start(bf16[1024,512]{1,0:T(8,128)(2,1)} %copy-done.8) | copy-start | bytes 3145732
  63.6 2.8 %copy-start.11 = (bf16[1024,512]{1,0:T(8,128)(2,1)S(1)}, bf16[1024,512]{1,0:T(8,128)(2,1)}, u32[]{:S(2)}) copy-start(bf16[1024,512]{1,0:T(8,128)(2,1)} %copy-done.10) | copy-start | bytes 3145732
  70.1 13.9 %collective-permute-start.1 = (bf16[288,256]{1,0:T(8,128)(2,1)S(1)}, bf16[288,256]{1,0:T(8,128)(2,1)S(1)}, u32[]{:S(2)}, u32[]{:S(2)}) collective-permute-start(bf16[288,256]{1,0:T(8,128)(2,1)S(1)} %get-tuple-element.21), channel_id=1, source_target_pairs={{0,2},{1,67},{2,160},{3,193},{4,166},{5,199},{6,4},{7,69},{8,10},{... | collective-permute-start | bytes 442376 | tf_op jit(solution)/shard_map/ppermute | solution.py:314
  76.2 9.0 %collective-permute-start.2 = (bf16[288,256]{1,0:T(8,128)(2,1)S(1)}, bf16[288,256]{1,0:T(8,128)(2,1)S(1)}, u32[]{:S(2)}, u32[]{:S(2)}) collective-permute-start(bf16[288,256]{1,0:T(8,128)(2,1)S(1)} %get-tuple-element.22), channel_id=1, source_target_pairs={{0,1},{1,66},{2,163},{3,192},{4,165},{5,198},{6,7},{7,68},{8,9},{9... | collective-permute-start | bytes 442376 | tf_op jit(solution)/shard_map/ppermute | solution.py:314
  77.8 10.2 %collective-permute-start.3 = (bf16[288,256]{1,0:T(8,128)(2,1)S(1)}, bf16[288,256]{1,0:T(8,128)(2,1)S(1)}, u32[]{:S(2)}, u32[]{:S(2)}) collective-permute-start(bf16[288,256]{1,0:T(8,128)(2,1)S(1)} %get-tuple-element.23), channel_id=1, source_target_pairs={{0,3},{1,64},{2,161},{3,194},{4,167},{5,196},{6,5},{7,70},{8,11},{... | collective-permute-start | bytes 442376 | tf_op jit(solution)/shard_map/ppermute | solution.py:314
  80.7 12.4 %collective-permute-start.4 = (bf16[288,256]{1,0:T(8,128)(2,1)S(1)}, bf16[288,256]{1,0:T(8,128)(2,1)S(1)}, u32[]{:S(2)}, u32[]{:S(2)}) collective-permute-start(bf16[288,256]{1,0:T(8,128)(2,1)S(1)} %get-tuple-element.24), channel_id=1, source_target_pairs={{0,0},{1,65},{2,162},{3,195},{4,164},{5,197},{6,6},{7,71},{8,8},{9... | collective-permute-start | bytes 442376 | tf_op jit(solution)/shard_map/ppermute | solution.py:314
